TPU v7x, 32 devices: a whole 2x2x4 slice. The times are simulated.
32 devices in a mesh: dp: 2 (over core), expert: 16 (over z, y, x).
Axes of the slice: x: 2, y: 2, z: 4, core: 2. Of those that a mesh axis runs over, the one named last changes fastest.
Arguments:
- tokens: bfloat16 [4096, 2048], P(('dp', 'expert')), may hold values from -6 to 6
- out_grad: bfloat16 [4096, 2048], P(('dp', 'expert')), may hold values from -3 to 3
- expert_ids: int32 [4096, 1], P(('dp', 'expert')), may hold values from 0 to 7, as said below
- gate_fixed: int32 [4096, 1], P(('dp', 'expert')), may hold values from 8192 to 65535
- w_gate: bfloat16 [16, 2048, 384], P('expert', 'dp'), may hold values from -0.125 to 0.125
- w_up: bfloat16 [16, 2048, 384], P('expert', 'dp'), may hold values from -0.125 to 0.125
- w_down: bfloat16 [16, 384, 2048], P('expert', None, 'dp'), may hold values from -0.21875 to 0.21875
- m_gate: float32 [16, 2048, 384], P('expert', 'dp'), may hold values from -12 to 12
- m_up: float32 [16, 2048, 384], P('expert', 'dp'), may hold values from -12 to 12
- m_down: float32 [16, 384, 2048], P('expert', None, 'dp'), may hold values from -12 to 12
- v_gate: float32 [16, 2048, 384], P('expert', 'dp'), may hold values from 1 to 100
- v_up: float32 [16, 2048, 384], P('expert', 'dp'), may hold values from 1 to 100
- v_down: float32 [16, 384, 2048], P('expert', None, 'dp'), may hold values from 1 to 100
Outputs:
- input_grad: bfloat16 [4096, 2048], P(('dp', 'expert'))
- new_w_gate: bfloat16 [16, 2048, 384], P('expert', 'dp')
- new_w_up: bfloat16 [16, 2048, 384], P('expert', 'dp')
- new_w_down: bfloat16 [16, 384, 2048], P('expert', None, 'dp')
- new_m_gate: float32 [16, 2048, 384], P('expert', 'dp')
- new_m_up: float32 [16, 2048, 384], P('expert', 'dp')
- new_m_down: float32 [16, 384, 2048], P('expert', None, 'dp')
- new_v_gate: float32 [16, 2048, 384], P('expert', 'dp')
- new_v_up: float32 [16, 2048, 384], P('expert', 'dp')
- new_v_down: float32 [16, 384, 2048], P('expert', None, 'dp')
Inputs may be any that keep to these rules, and one draw needn't show every extreme that they name: `expert_ids`: in each aligned block of 128 tokens (the tokens of one device) one expert, the same in every block, is named exactly 32 times; every other expert is named at most 16 times, and some other expert exactly 16 times in every block.
All inputs are finite; a program needn't handle non-finite values.
Results may differ from a plain program's by a relative error of at most 0.024.
Values may be sent and summed in bfloat16 or wider, within the bound.
A program may use at most 128 MiB of HBM per device.

v0:
```python
import jax
import jax.numpy as jnp
from jax import lax
from jax.sharding import PartitionSpec as P

beta_one = 0.9
beta_two = 0.95
learn_rate = 0.002
decay_rate = 0.1
epsilon = 1e-08
bias_one = 1.0 - beta_one**20
bias_two = 1.0 - beta_two**20
fixed_scale = 1.0 / 65536.0


def swapped(block, axis, bit):
    count = lax.axis_size(axis)
    route = []
    for low in range(count):
        high = low | 1 << bit
        if high != low and high < count:
            route += [(low, high), (high, low)]
    return lax.ppermute(block, axis, route)


def adam_update(weight, gradient, moment_one, moment_two):
    weight_full = weight.astype(jnp.float32)
    first_new = beta_one * moment_one + (1.0 - beta_one) * gradient
    second_new = beta_two * moment_two + (1.0 - beta_two) * gradient * gradient
    update = (
        first_new / bias_one / (jnp.sqrt(second_new / bias_two) + epsilon)
        + decay_rate * weight_full
    )
    return ((weight_full - learn_rate * update).astype(jnp.bfloat16), first_new, second_new)


def expert_pass(flat_input, flat_cotangent, gate_mat, up_mat, down_mat):
    contract_last = (((1,), (1,)), ((), ()))
    gate_pre = jnp.dot(flat_input, gate_mat, preferred_element_type=jnp.float32)
    up_pre = jnp.dot(flat_input, up_mat, preferred_element_type=jnp.float32)
    sigmoid_gate = jax.nn.sigmoid(gate_pre)
    active = gate_pre * sigmoid_gate
    hidden = (active * up_pre).astype(jnp.bfloat16)
    hidden_cot = lax.dot_general(
        flat_cotangent, down_mat, contract_last, preferred_element_type=jnp.float32
    )
    grad_up = (hidden_cot * active).astype(jnp.bfloat16)
    grad_gate = (
        hidden_cot * up_pre * sigmoid_gate * (1.0 + gate_pre * (1.0 - sigmoid_gate))
    ).astype(jnp.bfloat16)
    row_grad = lax.dot_general(
        grad_gate, gate_mat, contract_last, preferred_element_type=jnp.float32
    ) + lax.dot_general(grad_up, up_mat, contract_last, preferred_element_type=jnp.float32)
    return (hidden, grad_gate, grad_up, row_grad)


def weight_terms(flat_input, flat_cotangent, pass_result):
    hidden, grad_gate, grad_up = (pass_result[0], pass_result[1], pass_result[2])
    gate_term = jnp.einsum("rk,rf->kf", flat_input, grad_gate, preferred_element_type=jnp.float32)
    up_term = jnp.einsum("rk,rf->kf", flat_input, grad_up, preferred_element_type=jnp.float32)
    down_term = jnp.einsum("rk,rf->kf", flat_cotangent, hidden, preferred_element_type=jnp.float32)
    return [gate_term, up_term, down_term]


def per_device(
    tokens,
    out_grad,
    expert_ids,
    gate_fixed,
    w_gate,
    w_up,
    w_down,
    m_gate,
    m_up,
    m_down,
    v_gate,
    v_up,
    v_down,
):
    tok_rows = tokens.shape[0]
    feature_dim = tokens.shape[1]
    groups = lax.axis_size("expert")
    experts_here = groups // 2
    hot_rows = tok_rows // 4
    device_index = lax.axis_index("expert")
    half_bit = device_index % 2
    token_scale = gate_fixed[:, 0].astype(jnp.float32) * fixed_scale
    cotangent = (out_grad.astype(jnp.float32) * token_scale[:, None]).astype(jnp.bfloat16)
    chosen = expert_ids[:, 0]
    onehot = (chosen[:, None] == jnp.arange(experts_here, dtype=jnp.int32)[None, :]).astype(
        jnp.int32
    )
    position = jnp.sum(jnp.cumsum(onehot, axis=0) * onehot, axis=1) - 1
    half_rows = hot_rows // 2
    slot_index = chosen * hot_rows + position
    slot_token = (
        jnp.full((experts_here * hot_rows,), tok_rows, jnp.int32)
        .at[slot_index]
        .set(jnp.arange(tok_rows, dtype=jnp.int32))
    )
    input_pad = jnp.concatenate([tokens, jnp.zeros((1, feature_dim), jnp.bfloat16)], axis=0)
    cotangent_pad = jnp.concatenate([cotangent, jnp.zeros((1, feature_dim), jnp.bfloat16)], axis=0)
    slot_input = jnp.take(input_pad, slot_token, axis=0)
    slot_cotangent = jnp.take(cotangent_pad, slot_token, axis=0)
    shape_both = (experts_here, 2, hot_rows, feature_dim)
    sent_input = jnp.broadcast_to(
        slot_input.reshape(experts_here, 1, hot_rows, feature_dim), shape_both
    ).reshape(groups, hot_rows, feature_dim)
    sent_cotangent = jnp.broadcast_to(
        slot_cotangent.reshape(experts_here, 1, hot_rows, feature_dim), shape_both
    ).reshape(groups, hot_rows, feature_dim)
    rows_input, rows_cotangent = (
        lax.all_to_all(sent_input, "expert", split_axis=0, concat_axis=0, tiled=True),
        lax.all_to_all(sent_cotangent, "expert", split_axis=0, concat_axis=0, tiled=True),
    )
    gathered = (
        lax.all_gather(w_gate, "dp", axis=1, tiled=True),
        lax.all_gather(w_up, "dp", axis=1, tiled=True),
        lax.all_gather(w_down, "dp", axis=2, tiled=True),
    )
    gate_mat = gathered[0][0]
    up_mat = gathered[1][0]
    down_mat = gathered[2][0]
    flat_input = rows_input.reshape(groups * hot_rows, feature_dim)
    flat_cotangent = rows_cotangent.reshape(groups * hot_rows, feature_dim)
    own_pass = expert_pass(flat_input, flat_cotangent, gate_mat, up_mat, down_mat)
    partials = own_pass[3].reshape(groups, hot_rows, feature_dim)
    own_half = lax.dynamic_slice_in_dim(partials, half_bit * half_rows, half_rows, 1)
    other_half = lax.dynamic_slice_in_dim(partials, (1 - half_bit) * half_rows, half_rows, 1)
    pair_total = own_half + swapped(other_half, "expert", 0)
    returned = lax.all_to_all(
        pair_total.astype(jnp.bfloat16), "expert", split_axis=0, concat_axis=0, tiled=True
    )
    slot_grad = returned.reshape(experts_here * hot_rows, feature_dim)
    input_grad = jnp.take(slot_grad, slot_index, axis=0)
    summed = lax.psum_scatter(
        jnp.stack(weight_terms(flat_input, flat_cotangent, own_pass), axis=1),
        "dp",
        scatter_dimension=0,
        tiled=True,
    )
    gate_grad = summed[:, 0, :]
    up_grad = summed[:, 1, :]
    down_grad = summed[:, 2, :]
    gate_new, gate_first, gate_second = adam_update(w_gate[0], gate_grad, m_gate[0], v_gate[0])
    up_new, up_first, up_second = adam_update(w_up[0], up_grad, m_up[0], v_up[0])
    down_new, down_first, down_second = adam_update(w_down[0], down_grad.T, m_down[0], v_down[0])
    return (
        input_grad,
        gate_new[None],
        up_new[None],
        down_new[None],
        gate_first[None],
        up_first[None],
        down_first[None],
        gate_second[None],
        up_second[None],
        down_second[None],
    )


def solution(mesh):
    return jax.shard_map(
        per_device,
        mesh=mesh,
        in_specs=(
            P(("dp", "expert"), None),
            P(("dp", "expert"), None),
            P(("dp", "expert"), None),
            P(("dp", "expert"), None),
            P("expert", "dp", None),
            P("expert", "dp", None),
            P("expert", None, "dp"),
            P("expert", "dp", None),
            P("expert", "dp", None),
            P("expert", None, "dp"),
            P("expert", "dp", None),
            P("expert", "dp", None),
            P("expert", None, "dp"),
        ),
        out_specs=(
            P(("dp", "expert"), None),
            P("expert", "dp", None),
            P("expert", "dp", None),
            P("expert", None, "dp"),
            P("expert", "dp", None),
            P("expert", "dp", None),
            P("expert", None, "dp"),
            P("expert", "dp", None),
            P("expert", "dp", None),
            P("expert", None, "dp"),
        ),
        check_vma=False,
    )
```

profile of v0, /device:TPU:0, one launch (start us, length us, event | category | flops | bytes accessed | tf_op | source)
XLA Modules:
  0.0 252.1 jit_solution(10547356191957479043)
XLA Ops:
  15.7 1.6 broadcast_in_dim.59
  17.2 8.3 %all-to-all-start.1 = ((bf16[16,32,2048]{2,1,0:T(8,128)(2,1)}), bf16[16,32,2048]{2,1,0:T(8,128)(2,1)S(1)}, u32[]{:S(2)}, u32[]{:S(2)}) async-start(bf16[16,32,2048]{2,1,0:T(8,128)(2,1)} %bitcast.10), calls=%async_computation.1 | async-start | bytes 4194304 | tf_op jit(solution)/shard_map/all_to_all | solution.py:113
  26.3 42.3 %all-to-all-done.1 = bf16[16,32,2048]{2,1,0:T(8,128)(2,1)S(1)} async-done(((bf16[16,32,2048]{2,1,0:T(8,128)(2,1)}), bf16[16,32,2048]{2,1,0:T(8,128)(2,1)S(1)}, u32[]{:S(2)}, u32[]{:S(2)}) %all-to-all-start.1) | async-done | bytes 2097184 | tf_op jit(solution)/shard_map/all_to_all | solution.py:113
  68.6 1.8 broadcast_in_dim.57
  70.4 10.0 %all-to-all-start = ((bf16[16,32,2048]{2,1,0:T(8,128)(2,1)}), bf16[16,32,2048]{2,1,0:T(8,128)(2,1)}, u32[]{:S(2)}, u32[]{:S(2)}) async-start(bf16[16,32,2048]{2,1,0:T(8,128)(2,1)} %bitcast.6), calls=%async_computation | async-start | bytes 4194304 | tf_op jit(solution)/shard_map/all_to_all | solution.py:114
  82.2 3.5 %fusion.14 = f32[512,384]{1,0:T(8,128)} fusion(bf16[512,2048]{1,0:T(8,128)(2,1)S(1)} %bitcast.110, bf16[1,2048,384]{2,1,0:T(8,128)(2,1)} %all-gather.8.cloned.1.call-done), kind=kOutput, calls=%fused_computation.37 | convolution fusion | flops 805306368 | bytes 4456448 | tf_op jit(solution)/shard_map/dot_general | solution.py:39
  85.7 8.2 %all-gather.6.cloned.1.call-done = bf16[1,2048,384]{2,1,0:T(8,128)(2,1)} async-done(((bf16[1,1024,384]{2,1,0:T(8,128)(2,1)}), bf16[1,2048,384]{2,1,0:T(8,128)(2,1)}) %all-gather.6.cloned.1.call-update) | async-done | bytes 1572880 | tf_op jit(solution)/shard_map/all_gather | solution.py:118
  93.9 3.5 %fusion.17 = f32[512,384]{1,0:T(8,128)} fusion(bf16[512,2048]{1,0:T(8,128)(2,1)S(1)} %bitcast.111, bf16[1,2048,384]{2,1,0:T(8,128)(2,1)} %all-gather.6.cloned.1.call-done), kind=kOutput, calls=%fused_computation.40 | convolution fusion | flops 805306368 | bytes 4456448 | tf_op jit(solution)/shard_map/dot_general | solution.py:40
  97.4 25.5 %all-to-all-done = bf16[16,32,2048]{2,1,0:T(8,128)(2,1)} async-done(((bf16[16,32,2048]{2,1,0:T(8,128)(2,1)}), bf16[16,32,2048]{2,1,0:T(8,128)(2,1)}, u32[]{:S(2)}, u32[]{:S(2)}) %all-to-all-start) | async-done | bytes 2097184 | tf_op jit(solution)/shard_map/all_to_all | solution.py:114
  123.0 3.3 %convolution_bitcast_fusion = f32[2048,1,384]{2,0,1:T(8,128)S(1)} fusion(bf16[512,2048]{1,0:T(8,128)(2,1)} %bitcast.7, f32[512,384]{1,0:T(8,128)} %fusion.17, f32[512,384]{1,0:T(8,128)} %fusion.14), kind=kOutput, calls=%fused_computation.6 | convolution fusion | flops 806486016 | bytes 6815744 | tf_op jit(solution)/shard_map/rk,rf->kf/dot_general | solution.py:61
  126.4 4.0 %multiply_convert_fusion.2 = (bf16[512,384]{1,0:T(8,128)(2,1)S(1)}, bf16[512,384]{1,0:T(8,128)(2,1)S(1)}) fusion(f32[512,384]{1,0:T(8,128)} %fusion.14, f32[512,384]{1,0:T(8,128)} %fusion.17, bf16[512,2048]{1,0:T(8,128)(2,1)} %bitcast.7, bf16[1,384,2048]{2,1,0:T(8,128)(2,1)} %all-gather.4.cloned.1.call-done), kind=kOutput, calls=%fused_computation.50 | convolution fusion | flops 807862272 | bytes 6029312 | tf_op jit(solution)/shard_map/dot_general | solution.py:44
  133.0 4.3 %pad_maximum_fusion = f32[2048,3,384]{2,0,1:T(8,128)} fusion(f32[2048,1,384]{2,0,1:T(8,128)S(1)} %convolution_bitcast_fusion, f32[2048,1,384]{2,0,1:T(8,128)S(1)} %convolution_bitcast_fusion.1, f32[2048,1,384]{2,0,1:T(8,128)S(1)} %convolution_bitcast_fusion.2), kind=kLoop, calls=%fused_computation.4 | loop fusion | flops 4718592 | bytes 18874368 | tf_op jit(solution)/shard_map/stack | solution.py:137
  141.5 1.6 constant_dynamic-slice_fusion
  145.2 44.5 %collective-permute-done = f32[16,16,2048]{2,1,0:T(8,128)S(1)} collective-permute-done((f32[16,16,2048]{2,1,0:T(8,128)}, f32[16,16,2048]{2,1,0:T(8,128)S(1)}, u32[]{:S(2)}, u32[]{:S(2)}) %collective-permute-start) | collective-permute-done | bytes 2097184 | tf_op jit(solution)/shard_map/ppermute | solution.py:23
  189.7 2.8 %add_convert_fusion = bf16[16,16,2048]{2,1,0:T(8,128)(2,1)} fusion(f32[16,16,2048]{2,1,0:T(8,128)S(1)} %collective-permute-done, f32[16,32,2048]{2,1,0:T(8,128)} %bitcast.107, s32[]{:T(128)S(6)} %select_n.34), kind=kLoop, calls=%fused_computation.12 | loop fusion | flops 1048576 | bytes 5242884 | tf_op jit(solution)/shard_map/convert_element_type | solution.py:132
  192.5 11.1 %all-to-all-start.2 = ((bf16[16,16,2048]{2,1,0:T(8,128)(2,1)}), bf16[16,16,2048]{2,1,0:T(8,128)(2,1)S(1)}, u32[]{:S(2)}, u32[]{:S(2)}) async-start(bf16[16,16,2048]{2,1,0:T(8,128)(2,1)} %add_convert_fusion), calls=%async_computation.2 | async-start | bytes 2097152 | tf_op jit(solution)/shard_map/all_to_all | solution.py:131
  204.8 1.9 copy.25
  206.7 3.0 %copy.24 = f32[1,384,1024]{1,2,0:T(8,128)} copy(f32[1,384,1024]{2,1,0:T(8,128)} %param.24) | data formatting | bytes 3145728 | tf_op args[9]
  209.7 16.5 %all-to-all-done.2 = bf16[16,16,2048]{2,1,0:T(8,128)(2,1)S(1)} async-done(((bf16[16,16,2048]{2,1,0:T(8,128)(2,1)}), bf16[16,16,2048]{2,1,0:T(8,128)(2,1)S(1)}, u32[]{:S(2)}, u32[]{:S(2)}) %all-to-all-start.2) | async-done | bytes 1048608 | tf_op jit(solution)/shard_map/all_to_all | solution.py:131
  228.1 4.8 %fusion.24 = (f32[1,384,1024]{1,2,0:T(8,128)S(1)}, bf16[1,384,1024]{1,2,0:T(8,128)(2,1)}, f32[1,384,1024]{1,2,0:T(8,128)}) fusion(f32[1024,3,384]{2,0,1:T(8,128)} %reduce-scatter.2.cloned.1.call-done, f32[1,384,1024]{1,2,0:T(8,128)S(1)} %copy.25, f32[1,384,1024]{1,2,0:T(8,128)} %copy.24, bf16[1,384,1024]{1,2,0:T(8,128)(2,1)} %copy.23), kind=kLoop, calls=%fused_computation.57 | loop fusion | flops 6684672 | bytes 9437184 | tf_op jit(solution)/shard_map/broadcast_in_dim | solution.py:158
  232.9 2.4 copy.26
  235.3 1.6 copy.27
  236.9 1.6 copy.28
  238.5 7.1 %fusion.5 = (bf16[1,1024,384]{2,1,0:T(8,128)(2,1)}, f32[1,1024,384]{2,1,0:T(8,128)}, f32[1,1024,384]{2,1,0:T(8,128)}, bf16[1,1024,384]{2,1,0:T(8,128)(2,1)}, f32...) fusion(bf16[1,1024,384]{2,1,0:T(8,128)(2,1)S(1)} %copy-done.3, f32[1024,3,384]{2,0,1:T(8,128)} %reduce-scatter.2.cloned.1.call-done, ...), kind=kLoop, calls=%fused_computation.24 | loop fusion | flops 13369344 | bytes 18874368 | tf_op jit(solution)/shard_map/convert_element_type | solution.py:34
  (60 shorter events, 22.7 us)
Async XLA Ops:
  7.2 5.4 %copy-start.9 = (bf16[128,2048]{1,0:T(8,128)(2,1)S(1)}, bf16[128,2048]{1,0:T(8,128)(2,1)}, u32[]{:S(2)}) copy-start(bf16[128,2048]{1,0:T(8,128)(2,1)} %param.15) | copy-start | bytes 1572868
  17.2 51.4 %all-to-all-start.1 = ((bf16[16,32,2048]{2,1,0:T(8,128)(2,1)}), bf16[16,32,2048]{2,1,0:T(8,128)(2,1)S(1)}, u32[]{:S(2)}, u32[]{:S(2)}) async-start(bf16[16,32,2048]{2,1,0:T(8,128)(2,1)} %bitcast.10), calls=%async_computation.1 | async-start | bytes 4194304 | tf_op jit(solution)/shard_map/all_to_all | solution.py:113
  25.6 56.6 %all-gather.8.cloned.1.call-start = ((), (), s32[]{:S(2)}) async-start(), calls=%async_computation.6 | async-start | bytes 2359296 | tf_op jit(solution)/shard_map/all_gather | solution.py:117
  68.6 25.3 %copy-start.5 = (bf16[16,32,2048]{2,1,0:T(8,128)(2,1)}, bf16[16,32,2048]{2,1,0:T(8,128)(2,1)S(1)}, u32[]{:S(2)}) copy-start(bf16[16,32,2048]{2,1,0:T(8,128)(2,1)S(1)} %all-to-all-done.1) | copy-start | bytes 6291460
  70.4 52.6 %all-to-all-start = ((bf16[16,32,2048]{2,1,0:T(8,128)(2,1)}), bf16[16,32,2048]{2,1,0:T(8,128)(2,1)}, u32[]{:S(2)}, u32[]{:S(2)}) async-start(bf16[16,32,2048]{2,1,0:T(8,128)(2,1)} %bitcast.6), calls=%async_computation | async-start | bytes 4194304 | tf_op jit(solution)/shard_map/all_to_all | solution.py:114
  80.4 13.5 %all-gather.6.cloned.1.call-start = ((), (), s32[]{:S(2)}) async-start(), calls=%async_computation.5 | async-start | bytes 2359296 | tf_op jit(solution)/shard_map/all_gather | solution.py:118
  81.2 45.2 %all-gather.4.cloned.1.call-start = ((), (), s32[]{:S(2)}) async-start(), calls=%async_computation.4 | async-start | bytes 2359296 | tf_op jit(solution)/shard_map/all_gather | solution.py:119
  81.9 146.2 %reduce-scatter.2.cloned.1.call-start = ((), (), s32[]{:S(2)}) async-start(), calls=%async_computation.7 | async-start | bytes 14155776 | tf_op jit(solution)/shard_map/reduce_scatter | solution.py:136
  126.3 4.1 %copy-start.6 = (bf16[16,32,2048]{2,1,0:T(8,128)(2,1)S(1)}, bf16[16,32,2048]{2,1,0:T(8,128)(2,1)}, u32[]{:S(2)}) copy-start(bf16[16,32,2048]{2,1,0:T(8,128)(2,1)} %copy-done.5) | copy-start | bytes 6291460
  130.4 1.3 copy-start.10
  137.3 1.4 copy-start.7
  138.7 1.4 copy-start.8
  138.7 1.5 copy-start.11
  141.5 2.6 %copy-start = (f32[512,2048]{1,0:T(8,128)}, f32[512,2048]{1,0:T(8,128)S(1)}, u32[]{:S(2)}) copy-start(f32[512,2048]{1,0:T(8,128)S(1)} %convolution_add_fusion) | copy-start | bytes 12582916
  144.1 45.6 %collective-permute-start = (f32[16,16,2048]{2,1,0:T(8,128)}, f32[16,16,2048]{2,1,0:T(8,128)S(1)}, u32[]{:S(2)}, u32[]{:S(2)}) collective-permute-start(f32[16,16,2048]{2,1,0:T(8,128)} %constant_dynamic-slice_fusion), channel_id=1, source_target_pairs={{0,1},{1,0},{2,3},{3,2},{4,5},{5,4},{6,7},{7,6},{8,9},{9,8},{10,11... | collective-permute-start | bytes 6291464 | tf_op jit(solution)/shard_map/ppermute | solution.py:23
  192.5 11.1 %copy-start.4 = (bf16[1,384,1024]{2,1,0:T(8,128)(2,1)S(1)}, bf16[1,384,1024]{2,1,0:T(8,128)(2,1)}, u32[]{:S(2)}) copy-start(bf16[1,384,1024]{2,1,0:T(8,128)(2,1)} %param.21) | copy-start | bytes 2359300
  192.5 33.7 %all-to-all-start.2 = ((bf16[16,16,2048]{2,1,0:T(8,128)(2,1)}), bf16[16,16,2048]{2,1,0:T(8,128)(2,1)S(1)}, u32[]{:S(2)}, u32[]{:S(2)}) async-start(bf16[16,16,2048]{2,1,0:T(8,128)(2,1)} %add_convert_fusion), calls=%async_computation.2 | async-start | bytes 2097152 | tf_op jit(solution)/shard_map/all_to_all | solution.py:131
  232.9 2.4 copy-start.1
  236.9 1.6 copy-start.2
  236.9 1.6 copy-start.3
Sparse Core Ops, SparseCore 0:
  27.9 11.0 all-gather.7
  82.8 11.0 all-gather.5
  95.4 10.9 all-gather.3
  137.5 21.9 reduce-scatter.1
where the time goes:
time: 253 us; the launch traced here: 252 us
  waiting for transfers between devices  139 us (55%)
  starting transfers between devices  30.9 us (12%)
  other arithmetic  24.5 us (10%)
  local copies, waits for them, and re-layouts  23.9 us (9%)
  matrix products  19.7 us (8%)
  between operations  14 us (6%)
    ppermute x1, waiting for transfers between devices, swapped(): return lax.ppermute(block, axis, route)  44.5 us
    all_to_all x1, waiting for transfers between devices, per_device(): lax.all_to_all(sent_input, 'expert', split_axis=0, concat_axis=0, tiled=T...  42.3 us
    all_to_all x1, waiting for transfers between devices, per_device(): lax.all_to_all(sent_cotangent, 'expert', split_axis=0, concat_axis=0, til...  25.5 us
    all_to_all x1, waiting for transfers between devices, per_device(): lax.all_to_all(pair_total.astype(jnp.bfloat16), 'expert', split_axis=0, c...  16.5 us
    unnamed x30, local copies, waits for them, and re-layouts  14.3 us
    all_to_all x1, starting transfers between devices, per_device(): lax.all_to_all(pair_total.astype(jnp.bfloat16), 'expert', split_axis=0, c...  11.1 us
    all_to_all x1, starting transfers between devices, per_device(): lax.all_to_all(sent_cotangent, 'expert', split_axis=0, concat_axis=0, til...  10 us
    all_to_all x1, starting transfers between devices, per_device(): lax.all_to_all(sent_input, 'expert', split_axis=0, concat_axis=0, tiled=T...  8.31 us
  transfers between devices with their start and end apart: 8, of which 5 were waited for; matrix products, arithmetic and copies ran while one was open for 11% of the time, Pallas kernels for 0%

commit v1 on v0

v1 whole, which is shorter than its diff:
```python
import functools

import jax
import jax.numpy as jnp
from jax import lax
from jax.experimental import pallas as pl
from jax.experimental.pallas import tpu as pltpu
from jax.sharding import PartitionSpec as P

beta_one = 0.9
beta_two = 0.95
learn_rate = 0.002
decay_rate = 0.1
epsilon = 1e-08
bias_one = 1.0 - beta_one**20
bias_two = 1.0 - beta_two**20
fixed_scale = 1.0 / 65536.0

f32 = jnp.float32
bf16 = jnp.bfloat16
MESH = pl.DeviceIdType.MESH
lhs_t = (((0,), (0,)), ((), ()))
rhs_t = (((1,), (1,)), ((), ()))


def adam_update(weight, gradient, moment_one, moment_two):
    weight_full = weight.astype(f32)
    first_new = beta_one * moment_one + (1.0 - beta_one) * gradient
    second_new = beta_two * moment_two + (1.0 - beta_two) * gradient * gradient
    update = (
        first_new / bias_one / (jnp.sqrt(second_new / bias_two) + epsilon)
        + decay_rate * weight_full
    )
    return ((weight_full - learn_rate * update).astype(bf16), first_new, second_new)


def flipped(index, mask, count):
    total, bit = 0, 1
    while bit < count:
        here = lax.rem(lax.div(index, bit), 2)
        total = total + (1 - here if mask & bit else here) * bit
        bit *= 2
    return total


def remote(src, dst, send, recv, where):
    return pltpu.make_async_remote_copy(
        src_ref=src, dst_ref=dst, send_sem=send, recv_sem=recv, device_id=where, device_id_type=MESH
    )


def kernel(
    n, experts, hot, bs,
    tok_ref, og_ref, ids_ref, fix_ref, wg_ref, wu_ref, wd_ref,
    grad_ref, gate_out, up_out, down_out,
    slots, rows, gu, dn, part, psend, precv, rsend, ret, inner, hid, gu_grad, dn_grad,
    gu_recv, dn_recv, pick,
    wl, ws, wr, d_send, d_recv, f_send, f_recv, p_send, p_recv, r_send, r_recv, g_send, g_recv,
):
    tok_rows, depth = tok_ref.shape
    ff = wg_ref.shape[2]
    dpart = depth // n
    nb = dpart // bs
    all_rows = experts * hot
    d = lax.axis_index("dp")
    g = lax.axis_index("expert")
    e = lax.div(g, 2)
    s = lax.rem(g, 2)
    partner = g + 1 - 2 * s
    near, far = range(experts // 2), range(experts // 2, experts)
    order = [k for pair in zip(near, far) for k in pair]

    def peer(k):
        return {"expert": 2 * flipped(e, k, experts) + s}

    def dp_at(k):
        return lax.rem(d + k, n)

    def places(owner):
        at = pl.ds(pl.multiple_of(owner * dpart, dpart), dpart)
        return [gu.at[at, pl.ds(0, ff)], gu.at[at, pl.ds(ff, ff)], dn.at[:, at]]

    weights = [wg_ref.at[0], wu_ref.at[0], wd_ref.at[0]]
    local = [pltpu.make_async_copy(w, to, wl.at[i]) for i, (w, to) in enumerate(zip(weights, places(d)))]
    for copy in local:
        copy.start()

    barrier = pltpu.get_barrier_semaphore()
    for k in range(1, experts):
        pl.semaphore_signal(barrier, inc=1, device_id=peer(k), device_id_type=MESH)
    pl.semaphore_signal(barrier, inc=1, device_id={"expert": partner}, device_id_type=MESH)
    for k in range(1, n):
        pl.semaphore_signal(barrier, inc=1, device_id={"dp": dp_at(k)}, device_id_type=MESH)

    ids = ids_ref[...]
    chosen = ids == lax.broadcasted_iota(jnp.int32, (tok_rows, experts), 1)
    onehot = chosen.astype(f32)
    before = lax.broadcasted_iota(jnp.int32, (tok_rows, tok_rows), 1) < lax.broadcasted_iota(
        jnp.int32, (tok_rows, tok_rows), 0
    )
    counts = jnp.dot(before.astype(f32).astype(bf16), onehot.astype(bf16), preferred_element_type=f32)
    position = jnp.sum(counts * onehot, axis=1, keepdims=True)
    slot = ids.astype(f32) * hot + position
    lanes = lax.broadcasted_iota(jnp.int32, (tok_rows, all_rows), 1).astype(f32)
    chosen_slot = jnp.where(slot == lanes, 1.0, 0.0).astype(f32)
    pick[...] = chosen_slot.astype(bf16)
    scale = fix_ref[...].astype(f32) * fixed_scale
    cot = (og_ref[...].astype(f32) * scale).astype(bf16)
    for a, source in ((0, tok_ref[...]), (1, cot)):
        moved = lax.dot_general(pick[...], source, lhs_t, preferred_element_type=f32)
        slots[a] = moved.astype(bf16).reshape(experts, hot, depth)

    pl.semaphore_wait(barrier, experts + n - 1)

    sends = []

    def go(copy):
        copy.start()
        sends.append(copy)

    for pos, k in enumerate(order):
        for a in range(2):
            if k == 0:
                rows[a, 0, pos] = slots[a, e]
                go(remote(rows.at[a, 0, pos], rows.at[a, 1, pos], f_send.at[a, pos], f_recv.at[a, pos],
                          {"expert": partner}))
            else:
                go(remote(slots.at[a, flipped(e, k, experts)], rows.at[a, 0, pos], d_send.at[a, pos],
                          d_recv.at[a, pos], peer(k)))
    for k in range(1, n):
        for i in range(3):
            go(remote(weights[i], places(d)[i], ws.at[k - 1, i], wr.at[k - 1, i], {"dp": dp_at(k)}))

    for pos, k in enumerate(order):
        if k == 0:
            continue
        for a in range(2):
            remote(rows.at[a, 0, pos], rows.at[a, 0, pos], d_send.at[a, pos], d_recv.at[a, pos],
                   peer(k)).wait_recv()
            go(remote(rows.at[a, 0, pos], rows.at[a, 1, pos], f_send.at[a, pos], f_recv.at[a, pos],
                      {"expert": partner}))

    for copy in local:
        copy.wait()
    for k in range(1, n):
        arriving = places(lax.rem(d + n - k, n))
        for i in range(3):
            remote(arriving[i], arriving[i], ws.at[k - 1, i], wr.at[k - 1, i], {"dp": dp_at(k)}).wait_recv()

    def through(b, lo, many):
        here = pl.ds(lo, many)
        x = rows[0, b, here].reshape(many * hot, depth)
        c = rows[1, b, here].reshape(many * hot, depth)
        pre = jnp.dot(x, gu[...], preferred_element_type=f32)
        hidden_cot = lax.dot_general(c, dn[...], rhs_t, preferred_element_type=f32)
        gate_pre, up_pre = pre[:, :ff], pre[:, ff:]
        sig = jax.nn.sigmoid(gate_pre)
        active = gate_pre * sig
        at = pl.ds(b * all_rows + lo * hot, many * hot)
        hid[at] = (active * up_pre).astype(bf16)
        inner[at, pl.ds(ff, ff)] = (hidden_cot * active).astype(bf16)
        inner[at, pl.ds(0, ff)] = (hidden_cot * up_pre * sig * (1.0 + gate_pre * (1.0 - sig))).astype(bf16)
        return lax.dot_general(inner[at], gu[...], rhs_t, preferred_element_type=f32).reshape(many, hot, depth)

    part[...] = through(0, 0, experts)
    half = experts // 2
    for lo in (0, half):
        for pos in range(lo, lo + half):
            for a in range(2):
                remote(rows.at[a, 1, pos], rows.at[a, 1, pos], f_send.at[a, pos], f_recv.at[a, pos],
                       {"expert": partner}).wait_recv()
        psend[pl.ds(lo, half)] = through(1, lo, half).astype(bf16)
        for pos in range(lo, lo + half):
            go(remote(psend.at[pos], precv.at[pos], p_send.at[pos], p_recv.at[pos], {"expert": partner}))

    def weight_block(i, carry):
        block = lax.rem((d + 1) * nb + i, n * nb)
        at = pl.ds(pl.multiple_of(block * bs, bs), bs)
        x = rows[0, :, :, :, at].reshape(2 * all_rows, bs)
        c = rows[1, :, :, :, at].reshape(2 * all_rows, bs)
        gu_grad[block] = lax.dot_general(x, inner[...], lhs_t, preferred_element_type=f32)
        dn_grad[block] = lax.dot_general(hid[...], c, lhs_t, preferred_element_type=f32)
        return carry

    lax.fori_loop(0, (n - 1) * nb, weight_block, 0)
    for k in range(1, n):
        theirs = pl.ds(dp_at(k) * nb, nb)
        go(remote(gu_grad.at[theirs], gu_recv.at[k - 1], g_send.at[k - 1, 0], g_recv.at[k - 1, 0], {"dp": dp_at(k)}))
        go(remote(dn_grad.at[theirs], dn_recv.at[k - 1], g_send.at[k - 1, 1], g_recv.at[k - 1, 1], {"dp": dp_at(k)}))

    def give_back(pos):
        k = order[pos]
        remote(precv.at[pos], precv.at[pos], p_send.at[pos], p_recv.at[pos], {"expert": partner}).wait_recv()
        total = (part[pos] + precv[pos].astype(f32)).astype(bf16)
        if k == 0:
            ret[e] = total
        else:
            rsend[pos] = total
            go(remote(rsend.at[pos], ret.at[e], r_send.at[pos], r_recv.at[pos], peer(k)))

    for pos in range(half):
        give_back(pos)
    lax.fori_loop((n - 1) * nb, n * nb, weight_block, 0)
    for pos in range(half, experts):
        give_back(pos)

    for k in range(1, n):
        remote(gu_recv.at[k - 1], gu_recv.at[k - 1], g_send.at[k - 1, 0], g_recv.at[k - 1, 0],
               {"dp": dp_at(k)}).wait_recv()
        remote(dn_recv.at[k - 1], dn_recv.at[k - 1], g_send.at[k - 1, 1], g_recv.at[k - 1, 1],
               {"dp": dp_at(k)}).wait_recv()
    for i in range(nb):
        at = pl.ds(i * bs, bs)
        both = gu_grad[d * nb + i]
        down = dn_grad[d * nb + i]
        for k in range(1, n):
            both = both + gu_recv[k - 1, i]
            down = down + dn_recv[k - 1, i]
        gate_out[at] = both[:, :ff]
        up_out[at] = both[:, ff:]
        down_out[:, at] = down

    for pos, k in enumerate(order):
        if k:
            at = ret.at[flipped(e, k, experts)]
            remote(at, at, r_send.at[pos], r_recv.at[pos], peer(k)).wait_recv()
    back = ret[...].reshape(all_rows, depth)
    grad_ref[...] = jnp.dot(pick[...], back, preferred_element_type=f32).astype(bf16)
    for copy in sends:
        copy.wait_send()


def expert_layer(n, groups, tokens, out_grad, expert_ids, gate_fixed, w_gate, w_up, w_down):
    tok_rows, depth = tokens.shape
    ff = w_gate.shape[2]
    experts = groups // 2
    hot = tok_rows // 4
    dpart = depth // n
    bs = min(dpart, 512)
    nb = dpart // bs
    all_rows = experts * hot
    vmem = pl.BlockSpec(memory_space=pltpu.VMEM)
    hbm = pl.BlockSpec(memory_space=pl.ANY)
    dma = pltpu.SemaphoreType.DMA
    chunk = (experts, hot, depth)
    return pl.pallas_call(
        functools.partial(kernel, n, experts, hot, bs),
        out_shape=(
            jax.ShapeDtypeStruct((tok_rows, depth), bf16),
            jax.ShapeDtypeStruct((dpart, ff), f32),
            jax.ShapeDtypeStruct((dpart, ff), f32),
            jax.ShapeDtypeStruct((ff, dpart), f32),
        ),
        in_specs=[vmem] * 4 + [hbm] * 3,
        out_specs=(vmem,) * 4,
        scratch_shapes=[
            pltpu.VMEM((2,) + chunk, bf16),
            pltpu.VMEM((2, 2) + chunk, bf16),
            pltpu.VMEM((depth, 2 * ff), bf16),
            pltpu.VMEM((ff, depth), bf16),
            pltpu.VMEM(chunk, f32),
            pltpu.VMEM(chunk, bf16),
            pltpu.VMEM(chunk, bf16),
            pltpu.VMEM(chunk, bf16),
            pltpu.VMEM(chunk, bf16),
            pltpu.VMEM((2 * all_rows, 2 * ff), bf16),
            pltpu.VMEM((2 * all_rows, ff), bf16),
            pltpu.VMEM((n * nb, bs, 2 * ff), f32),
            pltpu.VMEM((n * nb, ff, bs), f32),
            pltpu.VMEM((n - 1, nb, bs, 2 * ff), f32),
            pltpu.VMEM((n - 1, nb, ff, bs), f32),
            pltpu.VMEM((tok_rows, all_rows), bf16),
            dma((3,)),
            dma((n - 1, 3)),
            dma((n - 1, 3)),
            dma((2, experts)),
            dma((2, experts)),
            dma((2, experts)),
            dma((2, experts)),
            dma((experts,)),
            dma((experts,)),
            dma((experts,)),
            dma((experts,)),
            dma((n - 1, 2)),
            dma((n - 1, 2)),
        ],
        compiler_params=pltpu.CompilerParams(
            collective_id=0, has_side_effects=True, vmem_limit_bytes=60 * 1024 * 1024
        ),
        name="expert_layer",
    )(tokens, out_grad, expert_ids, gate_fixed, w_gate, w_up, w_down)


def per_device(
    tokens,
    out_grad,
    expert_ids,
    gate_fixed,
    w_gate,
    w_up,
    w_down,
    m_gate,
    m_up,
    m_down,
    v_gate,
    v_up,
    v_down,
):
    n = lax.axis_size("dp")
    groups = lax.axis_size("expert")
    input_grad, gate_grad, up_grad, down_grad = expert_layer(
        n, groups, tokens, out_grad, expert_ids, gate_fixed, w_gate, w_up, w_down
    )
    gate_new, gate_first, gate_second = adam_update(w_gate[0], gate_grad, m_gate[0], v_gate[0])
    up_new, up_first, up_second = adam_update(w_up[0], up_grad, m_up[0], v_up[0])
    down_new, down_first, down_second = adam_update(w_down[0], down_grad, m_down[0], v_down[0])
    return (
        input_grad,
        gate_new[None],
        up_new[None],
        down_new[None],
        gate_first[None],
        up_first[None],
        down_first[None],
        gate_second[None],
        up_second[None],
        down_second[None],
    )


def solution(mesh):
    return jax.shard_map(
        per_device,
        mesh=mesh,
        in_specs=(
            P(("dp", "expert"), None),
            P(("dp", "expert"), None),
            P(("dp", "expert"), None),
            P(("dp", "expert"), None),
            P("expert", "dp", None),
            P("expert", "dp", None),
            P("expert", None, "dp"),
            P("expert", "dp", None),
            P("expert", "dp", None),
            P("expert", None, "dp"),
            P("expert", "dp", None),
            P("expert", "dp", None),
            P("expert", None, "dp"),
        ),
        out_specs=(
            P(("dp", "expert"), None),
            P("expert", "dp", None),
            P("expert", "dp", None),
            P("expert", None, "dp"),
            P("expert", "dp", None),
            P("expert", "dp", None),
            P("expert", None, "dp"),
            P("expert", "dp", None),
            P("expert", "dp", None),
            P("expert", None, "dp"),
        ),
        check_vma=False,
    )
```

time: 253 us -> 113 us (0.45)
  waiting for transfers between devices: 139 us -> 0 us
  Pallas kernels: 0 us -> 98.1 us
  starting transfers between devices: 30.9 us -> 0 us
  local copies, waits for them, and re-layouts: 23.9 us -> 3.63 us
  matrix products: 19.7 us -> 0 us
  other arithmetic: 24.5 us -> 9.98 us
  between operations: 14 us -> 0.73 us
    pallas_call x0 -> x1, Pallas kernels: none -> 98.1 us  [expert_layer(): pl.pallas_call(functools.partial(kernel, n, experts, hot, bs), out_shape=...]
    all_to_all x3 -> x0, waiting for transfers between devices: 84.4 us -> none  [the longest x1 42.3 us: per_device(): lax.all_to_all(sent_input, 'expert', split_axis=0, concat_axis=0, tiled=T...]
    ppermute x1 -> x0, waiting for transfers between devices: 44.5 us -> none  [swapped(): return lax.ppermute(block, axis, route)]
    all_to_all x3 -> x0, starting transfers between devices: 29.4 us -> none  [the longest x1 11.1 us: per_device(): lax.all_to_all(pair_total.astype(jnp.bfloat16), 'expert', split_axis=0, c...]
    dot_general x8 -> x0, matrix products: 19.7 us -> none  [the longest x1 4.04 us: expert_pass(): lax.dot_general(flat_cotangent, down_mat, contract_last, preferred_elemen...]
    convert_element_type x4 -> x0, other arithmetic: 11.9 us -> none  [the longest x1 7.09 us: adam_update(): (weight_full - learn_rate * update).astype(jnp.bfloat16)]
    unnamed x30 -> x19, local copies, waits for them, and re-layouts: 14.3 us -> 3.63 us
    all_gather x3 -> x0, waiting for transfers between devices: 8.23 us -> none  [the longest x1 8.19 us: per_device(): lax.all_gather(w_up, 'dp', axis=1, tiled=True)]
  transfers between devices with their start and end apart: 8 -> 0, of which waited for: 5 -> 0; matrix products, arithmetic and copies ran while one was open for 11% -> 0% of each run, Pallas kernels for 0% -> 0%
where the time goes in v1:
time: 113 us; the launch traced here: 112 us
  Pallas kernels  98.1 us (87%)
  other arithmetic  9.98 us (9%)
  local copies, waits for them, and re-layouts  3.63 us (3%)
    pallas_call x1, Pallas kernels, expert_layer(): pl.pallas_call(functools.partial(kernel, n, experts, hot, bs), out_shape=...  98.1 us
    broadcast_in_dim x1, other arithmetic, per_device(): up_second[None]  6.75 us
    unnamed x19, local copies, waits for them, and re-layouts  3.63 us
    broadcast_in_dim x1, other arithmetic, per_device(): down_second[None]  3.23 us

profile of v1, /device:TPU:0, one launch (start us, length us, event | category | flops | bytes accessed | tf_op | source)
XLA Modules:
  0.0 112.5 jit_solution(9212003186390634762)
XLA Ops:
  0.6 1.4 %copy.23.ids_ref = s32[128,1]{1,0:T(8,128)} copy(s32[128,1]{0,1:T(1,128)} %param.15) | data formatting | bytes 1024 | tf_op args[2]
  2.0 1.4 %copy.24.fix_ref = s32[128,1]{1,0:T(8,128)} copy(s32[128,1]{0,1:T(1,128)} %param.16) | data formatting | bytes 1024 | tf_op args[3]
  3.4 0.0 copy-start
  3.4 0.0 copy-start.1
  3.4 0.0 copy-start.3
  3.4 98.1 %expert_layer.1 = (bf16[128,2048]{1,0:T(8,128)(2,1)}, f32[1024,384]{1,0:T(8,128)}, f32[1024,384]{1,0:T(8,128)}, f32[384,1024]{1,0:T(8,128)}) custom-call(bf16[128,2048]{1,0:T(8,128)(2,1)} %tok_ref.1, bf16[128,2048]{1,0:T(8,128)(2,1)} %og_ref.1, s32[128,1]{1,0:T(8,128)} %copy.23.ids_ref, s32[128,1]{1,0:T(8,128)} %copy.24.fix_ref, ...), custom_call_target="tpu_custom_call" | custom-call | tf_op jit(solution)/shard_map/expert_layer/pallas_call | solution.py:246
  101.6 0.0 copy-done
  101.6 0.0 copy-done.1
  101.6 0.0 copy-done.3
  101.6 0.0 copy-start.2
  101.6 0.0 copy-start.4
  101.6 0.0 copy-start.5
  101.6 0.0 copy-start.6
  101.6 6.8 %fusion.19 = (f32[1,1024,384]{2,1,0:T(8,128)}, bf16[1,1024,384]{2,1,0:T(8,128)(2,1)}, f32[1,1024,384]{2,1,0:T(8,128)}, f32[1,1024,384]{2,1,0:T(8,128)}, bf16[1,1...) fusion(f32[1024,384]{1,0:T(8,128)} %get-tuple-element.16, f32[1,1024,384]{2,1,0:T(8,128)S(1)} %copy-done.3, ...), kind=kLoop, calls=%fused_computation.31 | loop fusion | flops 13369344 | bytes 18874368 | tf_op jit(solution)/shard_map/broadcast_in_dim | solution.py:326
  108.4 0.0 copy-done.2
  108.4 0.0 copy-done.4
  108.4 0.0 copy-done.5
  108.4 0.0 copy-done.6
  108.4 0.0 copy-start.7
  108.4 3.2 %fusion.18 = (f32[1,384,1024]{2,1,0:T(8,128)}, bf16[1,384,1024]{2,1,0:T(8,128)(2,1)}, f32[1,384,1024]{2,1,0:T(8,128)}) fusion(f32[384,1024]{1,0:T(8,128)S(1)} %copy-done.6, f32[1,384,1024]{2,1,0:T(8,128)S(1)} %copy-done.4, f32[1,384,1024]{2,1,0:T(8,128)S(1)} %copy-done.5, bf16[1,384,1024]{2,1,0:T(8,128)(2,1)S(1)} %copy-done.2), kind=kLoop, calls=%fused_computation.30 | loop fusion | flops 6684672 | bytes 9437184 | tf_op jit(solution)/shard_map/broadcast_in_dim | solution.py:327
  111.7 0.0 copy-done.7
  111.7 0.8 copy.26
Async XLA Ops:
  3.4 98.1 %copy-start = (bf16[1,1024,384]{2,1,0:T(8,128)(2,1)S(1)}, bf16[1,1024,384]{2,1,0:T(8,128)(2,1)}, u32[]{:S(2)}) copy-start(bf16[1,1024,384]{2,1,0:T(8,128)(2,1)} %wg_ref.1) | copy-start | bytes 2359300
  3.4 98.1 %copy-start.1 = (bf16[1,1024,384]{2,1,0:T(8,128)(2,1)S(1)}, bf16[1,1024,384]{2,1,0:T(8,128)(2,1)}, u32[]{:S(2)}) copy-start(bf16[1,1024,384]{2,1,0:T(8,128)(2,1)} %wu_ref.1) | copy-start | bytes 2359300
  3.4 98.1 %copy-start.3 = (f32[1,1024,384]{2,1,0:T(8,128)S(1)}, f32[1,1024,384]{2,1,0:T(8,128)}, u32[]{:S(2)}) copy-start(f32[1,1024,384]{2,1,0:T(8,128)} %param.24) | copy-start | bytes 4718596
  101.6 6.8 %copy-start.2 = (bf16[1,384,1024]{2,1,0:T(8,128)(2,1)S(1)}, bf16[1,384,1024]{2,1,0:T(8,128)(2,1)}, u32[]{:S(2)}) copy-start(bf16[1,384,1024]{2,1,0:T(8,128)(2,1)} %wd_ref.1) | copy-start | bytes 2359300
  101.6 6.8 %copy-start.4 = (f32[1,384,1024]{2,1,0:T(8,128)S(1)}, f32[1,384,1024]{2,1,0:T(8,128)}, u32[]{:S(2)}) copy-start(f32[1,384,1024]{2,1,0:T(8,128)} %param.25) | copy-start | bytes 4718596
  101.6 6.8 %copy-start.5 = (f32[1,384,1024]{2,1,0:T(8,128)S(1)}, f32[1,384,1024]{2,1,0:T(8,128)}, u32[]{:S(2)}) copy-start(f32[1,384,1024]{2,1,0:T(8,128)} %param.22) | copy-start | bytes 4718596
  101.6 6.8 %copy-start.6 = (f32[384,1024]{1,0:T(8,128)S(1)}, f32[384,1024]{1,0:T(8,128)}, u32[]{:S(2)}) copy-start(f32[384,1024]{1,0:T(8,128)} %get-tuple-element.17) | copy-start | bytes 4718596
  108.4 3.2 %copy-start.7 = (bf16[128,2048]{1,0:T(8,128)(2,1)S(1)}, bf16[128,2048]{1,0:T(8,128)(2,1)}, u32[]{:S(2)}) copy-start(bf16[128,2048]{1,0:T(8,128)(2,1)} %get-tuple-element.40) | copy-start | bytes 1572868

commit v2 on v1

--- a/solution.py
+++ b/solution.py
@@ -1,4 +1,5 @@
 import functools
+import math
 
 import jax
 import jax.numpy as jnp
@@ -18,6 +19,7 @@
 
 f32 = jnp.float32
 bf16 = jnp.bfloat16
+spare_bytes = 6 * 1024 * 1024
 MESH = pl.DeviceIdType.MESH
 lhs_t = (((0,), (0,)), ((), ()))
 rhs_t = (((1,), (1,)), ((), ()))
@@ -67,8 +69,9 @@
     e = lax.div(g, 2)
     s = lax.rem(g, 2)
     partner = g + 1 - 2 * s
-    near, far = range(experts // 2), range(experts // 2, experts)
-    order = [k for pair in zip(near, far) for k in pair]
+    order = list(range(experts))
+    half = experts // 2
+    window = 3
 
     def peer(k):
         return {"expert": 2 * flipped(e, k, experts) + s}
@@ -93,21 +96,20 @@
         pl.semaphore_signal(barrier, inc=1, device_id={"dp": dp_at(k)}, device_id_type=MESH)
 
     ids = ids_ref[...]
-    chosen = ids == lax.broadcasted_iota(jnp.int32, (tok_rows, experts), 1)
-    onehot = chosen.astype(f32)
-    before = lax.broadcasted_iota(jnp.int32, (tok_rows, tok_rows), 1) < lax.broadcasted_iota(
-        jnp.int32, (tok_rows, tok_rows), 0
-    )
-    counts = jnp.dot(before.astype(f32).astype(bf16), onehot.astype(bf16), preferred_element_type=f32)
-    position = jnp.sum(counts * onehot, axis=1, keepdims=True)
+    onehot = (ids == lax.broadcasted_iota(jnp.int32, (experts, tok_rows), 0)).astype(f32)
+    row_at = lax.broadcasted_iota(jnp.int32, (tok_rows, tok_rows), 0)
+    col_at = lax.broadcasted_iota(jnp.int32, (tok_rows, tok_rows), 1)
+    before = jnp.where(row_at < col_at, 1.0, 0.0).astype(bf16)
+    counts = jnp.dot(onehot.astype(bf16), before, preferred_element_type=f32)
+    position = jnp.sum(counts * onehot, axis=0, keepdims=True)
     slot = ids.astype(f32) * hot + position
-    lanes = lax.broadcasted_iota(jnp.int32, (tok_rows, all_rows), 1).astype(f32)
-    chosen_slot = jnp.where(slot == lanes, 1.0, 0.0).astype(f32)
-    pick[...] = chosen_slot.astype(bf16)
-    scale = fix_ref[...].astype(f32) * fixed_scale
+    heights = lax.broadcasted_iota(jnp.int32, (all_rows, tok_rows), 0).astype(f32)
+    pick[...] = jnp.where(slot == heights, 1.0, 0.0).astype(bf16)
+    scale_row = fix_ref[...].astype(f32) * fixed_scale
+    scale = jnp.sum(jnp.where(row_at == col_at, scale_row, 0.0), axis=1, keepdims=True)
     cot = (og_ref[...].astype(f32) * scale).astype(bf16)
     for a, source in ((0, tok_ref[...]), (1, cot)):
-        moved = lax.dot_general(pick[...], source, lhs_t, preferred_element_type=f32)
+        moved = jnp.dot(pick[...], source, preferred_element_type=f32)
         slots[a] = moved.astype(bf16).reshape(experts, hot, depth)
 
     pl.semaphore_wait(barrier, experts + n - 1)
@@ -118,27 +120,37 @@
         copy.start()
         sends.append(copy)
 
-    for pos, k in enumerate(order):
+    def forward(a, pos):
+        go(remote(rows.at[a, 0, pos], rows.at[a, 1, pos], f_send.at[a, pos], f_recv.at[a, pos],
+                  {"expert": partner}))
+
+    def direct(a, pos):
+        k = order[pos]
+        go(remote(slots.at[a, flipped(e, k, experts)], rows.at[a, 0, pos], d_send.at[a, pos],
+                  d_recv.at[a, pos], peer(k)))
+
+    waiting = [(a, pos) for pos in range(half, experts) for a in range(2)]
+    for a, pos in waiting[:window]:
+        direct(a, pos)
+    for pos in range(1, half):
         for a in range(2):
-            if k == 0:
-                rows[a, 0, pos] = slots[a, e]
-                go(remote(rows.at[a, 0, pos], rows.at[a, 1, pos], f_send.at[a, pos], f_recv.at[a, pos],
-                          {"expert": partner}))
-            else:
-                go(remote(slots.at[a, flipped(e, k, experts)], rows.at[a, 0, pos], d_send.at[a, pos],
-                          d_recv.at[a, pos], peer(k)))
+            direct(a, pos)
+    for a in range(2):
+        rows[a, 0, 0] = slots[a, e]
+        forward(a, 0)
     for k in range(1, n):
         for i in range(3):
             go(remote(weights[i], places(d)[i], ws.at[k - 1, i], wr.at[k - 1, i], {"dp": dp_at(k)}))
 
-    for pos, k in enumerate(order):
-        if k == 0:
-            continue
+    started = window
+    for pos in range(1, experts):
         for a in range(2):
             remote(rows.at[a, 0, pos], rows.at[a, 0, pos], d_send.at[a, pos], d_recv.at[a, pos],
-                   peer(k)).wait_recv()
-            go(remote(rows.at[a, 0, pos], rows.at[a, 1, pos], f_send.at[a, pos], f_recv.at[a, pos],
-                      {"expert": partner}))
+                   peer(order[pos])).wait_recv()
+            if pos >= half and started < len(waiting):
+                direct(*waiting[started])
+                started += 1
+            forward(a, pos)
 
     for copy in local:
         copy.wait()
@@ -162,8 +174,6 @@
         inner[at, pl.ds(0, ff)] = (hidden_cot * up_pre * sig * (1.0 + gate_pre * (1.0 - sig))).astype(bf16)
         return lax.dot_general(inner[at], gu[...], rhs_t, preferred_element_type=f32).reshape(many, hot, depth)
 
-    part[...] = through(0, 0, experts)
-    half = experts // 2
     for lo in (0, half):
         for pos in range(lo, lo + half):
             for a in range(2):
@@ -173,20 +183,22 @@
         for pos in range(lo, lo + half):
             go(remote(psend.at[pos], precv.at[pos], p_send.at[pos], p_recv.at[pos], {"expert": partner}))
 
-    def weight_block(i, carry):
+    part[...] = through(0, 0, experts)
+
+    def weight_block(i):
         block = lax.rem((d + 1) * nb + i, n * nb)
         at = pl.ds(pl.multiple_of(block * bs, bs), bs)
         x = rows[0, :, :, :, at].reshape(2 * all_rows, bs)
         c = rows[1, :, :, :, at].reshape(2 * all_rows, bs)
         gu_grad[block] = lax.dot_general(x, inner[...], lhs_t, preferred_element_type=f32)
         dn_grad[block] = lax.dot_general(hid[...], c, lhs_t, preferred_element_type=f32)
-        return carry
-
-    lax.fori_loop(0, (n - 1) * nb, weight_block, 0)
-    for k in range(1, n):
-        theirs = pl.ds(dp_at(k) * nb, nb)
-        go(remote(gu_grad.at[theirs], gu_recv.at[k - 1], g_send.at[k - 1, 0], g_recv.at[k - 1, 0], {"dp": dp_at(k)}))
-        go(remote(dn_grad.at[theirs], dn_recv.at[k - 1], g_send.at[k - 1, 1], g_recv.at[k - 1, 1], {"dp": dp_at(k)}))
+        if i % nb == nb - 1 and i < (n - 1) * nb:
+            k = i // nb + 1
+            theirs = pl.ds(dp_at(k) * nb, nb)
+            go(remote(gu_grad.at[theirs], gu_recv.at[k - 1], g_send.at[k - 1, 0], g_recv.at[k - 1, 0],
+                      {"dp": dp_at(k)}))
+            go(remote(dn_grad.at[theirs], dn_recv.at[k - 1], g_send.at[k - 1, 1], g_recv.at[k - 1, 1],
+                      {"dp": dp_at(k)}))
 
     def give_back(pos):
         k = order[pos]
@@ -198,11 +210,13 @@
             rsend[pos] = total
             go(remote(rsend.at[pos], ret.at[e], r_send.at[pos], r_recv.at[pos], peer(k)))
 
-    for pos in range(half):
+    blocks = list(range(n * nb))
+    for pos in range(experts):
         give_back(pos)
-    lax.fori_loop((n - 1) * nb, n * nb, weight_block, 0)
-    for pos in range(half, experts):
-        give_back(pos)
+        if pos and blocks:
+            weight_block(blocks.pop(0))
+    for i in blocks:
+        weight_block(i)
 
     for k in range(1, n):
         remote(gu_recv.at[k - 1], gu_recv.at[k - 1], g_send.at[k - 1, 0], g_recv.at[k - 1, 0],
@@ -225,7 +239,7 @@
             at = ret.at[flipped(e, k, experts)]
             remote(at, at, r_send.at[pos], r_recv.at[pos], peer(k)).wait_recv()
     back = ret[...].reshape(all_rows, depth)
-    grad_ref[...] = jnp.dot(pick[...], back, preferred_element_type=f32).astype(bf16)
+    grad_ref[...] = lax.dot_general(pick[...], back, lhs_t, preferred_element_type=f32).astype(bf16)
     for copy in sends:
         copy.wait_send()
 
@@ -243,6 +257,26 @@
     hbm = pl.BlockSpec(memory_space=pl.ANY)
     dma = pltpu.SemaphoreType.DMA
     chunk = (experts, hot, depth)
+    buffers = [
+        pltpu.VMEM((2,) + chunk, bf16),
+        pltpu.VMEM((2, 2) + chunk, bf16),
+        pltpu.VMEM((depth, 2 * ff), bf16),
+        pltpu.VMEM((ff, depth), bf16),
+        pltpu.VMEM(chunk, f32),
+        pltpu.VMEM(chunk, bf16),
+        pltpu.VMEM(chunk, bf16),
+        pltpu.VMEM(chunk, bf16),
+        pltpu.VMEM(chunk, bf16),
+        pltpu.VMEM((2 * all_rows, 2 * ff), bf16),
+        pltpu.VMEM((2 * all_rows, ff), bf16),
+        pltpu.VMEM((n * nb, bs, 2 * ff), f32),
+        pltpu.VMEM((n * nb, ff, bs), f32),
+        pltpu.VMEM((n - 1, nb, bs, 2 * ff), f32),
+        pltpu.VMEM((n - 1, nb, ff, bs), f32),
+        pltpu.VMEM((all_rows, tok_rows), bf16),
+    ]
+    held = sum(math.prod(b.shape) * b.dtype.itemsize for b in buffers)
+    moved = 3 * tok_rows * depth * 2 + 3 * dpart * ff * 4
     return pl.pallas_call(
         functools.partial(kernel, n, experts, hot, bs),
         out_shape=(
@@ -253,23 +287,7 @@
         ),
         in_specs=[vmem] * 4 + [hbm] * 3,
         out_specs=(vmem,) * 4,
-        scratch_shapes=[
-            pltpu.VMEM((2,) + chunk, bf16),
-            pltpu.VMEM((2, 2) + chunk, bf16),
-            pltpu.VMEM((depth, 2 * ff), bf16),
-            pltpu.VMEM((ff, depth), bf16),
-            pltpu.VMEM(chunk, f32),
-            pltpu.VMEM(chunk, bf16),
-            pltpu.VMEM(chunk, bf16),
-            pltpu.VMEM(chunk, bf16),
-            pltpu.VMEM(chunk, bf16),
-            pltpu.VMEM((2 * all_rows, 2 * ff), bf16),
-            pltpu.VMEM((2 * all_rows, ff), bf16),
-            pltpu.VMEM((n * nb, bs, 2 * ff), f32),
-            pltpu.VMEM((n * nb, ff, bs), f32),
-            pltpu.VMEM((n - 1, nb, bs, 2 * ff), f32),
-            pltpu.VMEM((n - 1, nb, ff, bs), f32),
-            pltpu.VMEM((tok_rows, all_rows), bf16),
+        scratch_shapes=buffers + [
             dma((3,)),
             dma((n - 1, 3)),
             dma((n - 1, 3)),
@@ -285,7 +303,7 @@
             dma((n - 1, 2)),
         ],
         compiler_params=pltpu.CompilerParams(
-            collective_id=0, has_side_effects=True, vmem_limit_bytes=60 * 1024 * 1024
+            collective_id=0, has_side_effects=True, vmem_limit_bytes=held + moved + spare_bytes
         ),
         name="expert_layer",
     )(tokens, out_grad, expert_ids, gate_fixed, w_gate, w_up, w_down)
@@ -309,7 +327,7 @@
     n = lax.axis_size("dp")
     groups = lax.axis_size("expert")
     input_grad, gate_grad, up_grad, down_grad = expert_layer(
-        n, groups, tokens, out_grad, expert_ids, gate_fixed, w_gate, w_up, w_down
+        n, groups, tokens, out_grad, expert_ids.reshape(1, -1), gate_fixed.reshape(1, -1), w_gate, w_up, w_down
     )
     gate_new, gate_first, gate_second = adam_update(w_gate[0], gate_grad, m_gate[0], v_gate[0])
     up_new, up_first, up_second = adam_update(w_up[0], up_grad, m_up[0], v_up[0])

time: 113 us -> 114 us (level)
  the two profiles are of different devices: /device:TPU:0 before, /device:TPU:13 now
where the time goes in v2:
time: 114 us; the launch traced here: 113 us
  Pallas kernels  95.7 us (84%)
  other arithmetic  9.35 us (8%)
  local copies, waits for them, and re-layouts  7.6 us (7%)
    pallas_call x1, Pallas kernels, expert_layer(): pl.pallas_call(functools.partial(kernel, n, experts, hot, bs), out_shape=...  95.7 us
    unnamed x23, local copies, waits for them, and re-layouts  7.6 us
    broadcast_in_dim x1, other arithmetic, per_device(): up_second[None]  6.11 us
    broadcast_in_dim x1, other arithmetic, per_device(): down_second[None]  3.24 us

profile of v2, /device:TPU:13, one launch (start us, length us, event | category | flops | bytes accessed | tf_op | source)
XLA Modules:
  0.0 113.3 jit_solution(469028203212528735)
XLA Ops:
  0.6 0.0 copy-start
  0.7 1.1 copy-done
  1.8 0.0 copy-start.1
  1.8 1.1 copy-done.1
  2.9 0.0 copy-start.2
  2.9 1.1 copy-done.2
  4.0 0.0 copy-start.3
  4.0 1.0 copy-done.3
  5.1 0.0 copy-start.4
  5.1 1.0 copy-done.4
  6.1 0.0 copy-start.5
  6.1 0.7 copy-done.5
  6.8 0.0 copy-start.6
  6.8 0.7 copy-done.6
  7.4 95.7 %expert_layer.1 = (bf16[128,2048]{1,0:T(8,128)(2,1)S(1)}, f32[1024,384]{1,0:T(8,128)S(1)}, f32[1024,384]{1,0:T(8,128)S(1)}, f32[384,1024]{1,0:T(8,128)S(1)}) custom-call(bf16[128,2048]{1,0:T(8,128)(2,1)S(1)} %copy-done.3, bf16[128,2048]{1,0:T(8,128)(2,1)S(1)} %copy-done.4, s32[1,128]{1,0:T(1,128)S(1)} %bitcast.71, s32[1,128]{1,0:T(1,128)S(1)} %bitcast.72, ...), custom_call_target="tpu_custom_call" | custom-call | tf_op jit(solution)/shard_map/expert_layer/pallas_call | solution.py:280
  103.1 0.0 copy-done.7
  103.2 0.0 copy-done.8
  103.2 0.0 copy-start.9
  103.2 0.0 copy-start.10
  103.2 6.1 %fusion.19 = (f32[1,1024,384]{2,1,0:T(8,128)}, bf16[1,1024,384]{2,1,0:T(8,128)(2,1)}, f32[1,1024,384]{2,1,0:T(8,128)}, f32[1,1024,384]{2,1,0:T(8,128)}, bf16[1,1...) fusion(f32[1024,384]{1,0:T(8,128)S(1)} %get-tuple-element.16, f32[1,1024,384]{2,1,0:T(8,128)S(1)} %copy-done.7, ...), kind=kLoop, calls=%fused_computation.31 | loop fusion | flops 13369344 | bytes 18874368 | tf_op jit(solution)/shard_map/broadcast_in_dim | solution.py:344
  109.3 0.0 copy-done.9
  109.3 0.0 copy-done.10
  109.3 3.2 %fusion.18 = (f32[1,384,1024]{2,1,0:T(8,128)}, bf16[1,384,1024]{2,1,0:T(8,128)(2,1)}, f32[1,384,1024]{2,1,0:T(8,128)}) fusion(f32[384,1024]{1,0:T(8,128)S(1)} %get-tuple-element.17, f32[1,384,1024]{2,1,0:T(8,128)S(1)} %copy-done.9, f32[1,384,1024]{2,1,0:T(8,128)S(1)} %copy-done.10, bf16[1,384,1024]{2,1,0:T(8,128)(2,1)S(1)} %copy-done.2), kind=kLoop, calls=%fused_computation.30 | loop fusion | flops 6684672 | bytes 9437184 | tf_op jit(solution)/shard_map/broadcast_in_dim | solution.py:345
  112.6 0.8 copy.24
  (2 shorter events, 0.0 us)
Async XLA Ops:
  0.6 1.1 %copy-start = (bf16[1,1024,384]{2,1,0:T(8,128)(2,1)S(1)}, bf16[1,1024,384]{2,1,0:T(8,128)(2,1)}, u32[]{:S(2)}) copy-start(bf16[1,1024,384]{2,1,0:T(8,128)(2,1)} %wg_ref.1) | copy-start | bytes 2359300
  1.8 1.1 copy-start.1
  2.9 1.1 copy-start.2
  4.0 1.0 copy-start.3
  5.1 1.0 copy-start.4
  6.1 0.7 copy-start.5
  6.8 0.7 copy-start.6
  7.4 95.7 %copy-start.7 = (f32[1,1024,384]{2,1,0:T(8,128)S(1)}, f32[1,1024,384]{2,1,0:T(8,128)}, u32[]{:S(2)}) copy-start(f32[1,1024,384]{2,1,0:T(8,128)} %param.24) | copy-start | bytes 4718596
  7.4 95.7 %copy-start.8 = (f32[1,1024,384]{2,1,0:T(8,128)S(1)}, f32[1,1024,384]{2,1,0:T(8,128)}, u32[]{:S(2)}) copy-start(f32[1,1024,384]{2,1,0:T(8,128)} %param.21) | copy-start | bytes 4718596
  103.2 6.1 %copy-start.9 = (f32[1,384,1024]{2,1,0:T(8,128)S(1)}, f32[1,384,1024]{2,1,0:T(8,128)}, u32[]{:S(2)}) copy-start(f32[1,384,1024]{2,1,0:T(8,128)} %param.25) | copy-start | bytes 4718596
  103.2 6.1 %copy-start.10 = (f32[1,384,1024]{2,1,0:T(8,128)S(1)}, f32[1,384,1024]{2,1,0:T(8,128)}, u32[]{:S(2)}) copy-start(f32[1,384,1024]{2,1,0:T(8,128)} %param.22) | copy-start | bytes 4718596

commit v3 on v2

--- a/solution.py
+++ b/solution.py
@@ -1,5 +1,4 @@
 import functools
-import math
 
 import jax
 import jax.numpy as jnp
@@ -19,7 +18,6 @@
 
 f32 = jnp.float32
 bf16 = jnp.bfloat16
-spare_bytes = 6 * 1024 * 1024
 MESH = pl.DeviceIdType.MESH
 lhs_t = (((0,), (0,)), ((), ()))
 rhs_t = (((1,), (1,)), ((), ()))
@@ -30,7 +28,7 @@
     first_new = beta_one * moment_one + (1.0 - beta_one) * gradient
     second_new = beta_two * moment_two + (1.0 - beta_two) * gradient * gradient
     update = (
-        first_new / bias_one / (jnp.sqrt(second_new / bias_two) + epsilon)
+        first_new * (1.0 / bias_one) / (jnp.sqrt(second_new * (1.0 / bias_two)) + epsilon)
         + decay_rate * weight_full
     )
     return ((weight_full - learn_rate * update).astype(bf16), first_new, second_new)
@@ -69,8 +67,12 @@
     e = lax.div(g, 2)
     s = lax.rem(g, 2)
     partner = g + 1 - 2 * s
-    order = list(range(experts))
     half = experts // 2
+    quarter = experts // 4
+    near, far = list(range(half)), list(range(half, experts))
+    order = near[:quarter] + far[:quarter] + near[quarter:] + far[quarter:]
+    place = {k: pos for pos, k in enumerate(order)}
+    arrivals = near[1:3] + far[:2] + near[3:] + far[2:]
     window = 3
 
     def peer(k):
@@ -129,12 +131,12 @@
         go(remote(slots.at[a, flipped(e, k, experts)], rows.at[a, 0, pos], d_send.at[a, pos],
                   d_recv.at[a, pos], peer(k)))
 
-    waiting = [(a, pos) for pos in range(half, experts) for a in range(2)]
+    waiting = [(a, place[k]) for k in far for a in range(2)]
     for a, pos in waiting[:window]:
         direct(a, pos)
-    for pos in range(1, half):
+    for k in near[1:]:
         for a in range(2):
-            direct(a, pos)
+            direct(a, place[k])
     for a in range(2):
         rows[a, 0, 0] = slots[a, e]
         forward(a, 0)
@@ -143,11 +145,12 @@
             go(remote(weights[i], places(d)[i], ws.at[k - 1, i], wr.at[k - 1, i], {"dp": dp_at(k)}))
 
     started = window
-    for pos in range(1, experts):
+    for k in arrivals:
+        pos = place[k]
         for a in range(2):
             remote(rows.at[a, 0, pos], rows.at[a, 0, pos], d_send.at[a, pos], d_recv.at[a, pos],
-                   peer(order[pos])).wait_recv()
-            if pos >= half and started < len(waiting):
+                   peer(k)).wait_recv()
+            if k >= half and started < len(waiting):
                 direct(*waiting[started])
                 started += 1
             forward(a, pos)
@@ -174,16 +177,14 @@
         inner[at, pl.ds(0, ff)] = (hidden_cot * up_pre * sig * (1.0 + gate_pre * (1.0 - sig))).astype(bf16)
         return lax.dot_general(inner[at], gu[...], rhs_t, preferred_element_type=f32).reshape(many, hot, depth)
 
-    for lo in (0, half):
+    def forwarded(lo):
         for pos in range(lo, lo + half):
             for a in range(2):
                 remote(rows.at[a, 1, pos], rows.at[a, 1, pos], f_send.at[a, pos], f_recv.at[a, pos],
                        {"expert": partner}).wait_recv()
         psend[pl.ds(lo, half)] = through(1, lo, half).astype(bf16)
-        for pos in range(lo, lo + half):
+        for pos in list(range(lo + quarter, lo + half)) + list(range(lo, lo + quarter)):
             go(remote(psend.at[pos], precv.at[pos], p_send.at[pos], p_recv.at[pos], {"expert": partner}))
-
-    part[...] = through(0, 0, experts)
 
     def weight_block(i):
         block = lax.rem((d + 1) * nb + i, n * nb)
@@ -211,9 +212,14 @@
             go(remote(rsend.at[pos], ret.at[e], r_send.at[pos], r_recv.at[pos], peer(k)))
 
     blocks = list(range(n * nb))
-    for pos in range(experts):
-        give_back(pos)
-        if pos and blocks:
+    forwarded(0)
+    part[...] = through(0, 0, experts)
+    for k in far[:quarter]:
+        give_back(place[k])
+    forwarded(half)
+    for k in near[1:quarter] + near[:1] + far[quarter:] + near[quarter:]:
+        give_back(place[k])
+        if blocks and k:
             weight_block(blocks.pop(0))
     for i in blocks:
         weight_block(i)
@@ -275,8 +281,6 @@
         pltpu.VMEM((n - 1, nb, ff, bs), f32),
         pltpu.VMEM((all_rows, tok_rows), bf16),
     ]
-    held = sum(math.prod(b.shape) * b.dtype.itemsize for b in buffers)
-    moved = 3 * tok_rows * depth * 2 + 3 * dpart * ff * 4
     return pl.pallas_call(
         functools.partial(kernel, n, experts, hot, bs),
         out_shape=(
@@ -303,7 +307,7 @@
             dma((n - 1, 2)),
         ],
         compiler_params=pltpu.CompilerParams(
-            collective_id=0, has_side_effects=True, vmem_limit_bytes=held + moved + spare_bytes
+            collective_id=0, has_side_effects=True, vmem_limit_bytes=60 * 1024 * 1024
         ),
         name="expert_layer",
     )(tokens, out_grad, expert_ids, gate_fixed, w_gate, w_up, w_down)

time: 114 us -> 104 us (0.912)
  the two profiles are of different devices: /device:TPU:13 before, /device:TPU:0 now
where the time goes in v3:
time: 104 us
  Pallas kernels  92.3 us (89%)
  other arithmetic  10.2 us (10%)
    pallas_call x1, Pallas kernels, expert_layer(): pl.pallas_call(functools.partial(kernel, n, experts, hot, bs), out_shape=...  92.3 us
    broadcast_in_dim x1, other arithmetic, per_device(): up_second[None]  6.93 us
    broadcast_in_dim x1, other arithmetic, per_device(): down_second[None]  3.23 us

profile of v3, /device:TPU:0, one launch (start us, length us, event | category | flops | bytes accessed | tf_op | source)
XLA Modules:
  0.0 104.0 jit_solution(16052852620627024461)
XLA Ops:
  0.6 0.0 copy-start
  0.7 0.0 copy-start.1
  0.7 0.0 copy-start.3
  0.7 92.3 %expert_layer.1 = (bf16[128,2048]{1,0:T(8,128)(2,1)}, f32[1024,384]{1,0:T(8,128)}, f32[1024,384]{1,0:T(8,128)}, f32[384,1024]{1,0:T(8,128)}) custom-call(bf16[128,2048]{1,0:T(8,128)(2,1)} %tok_ref.1, bf16[128,2048]{1,0:T(8,128)(2,1)} %og_ref.1, s32[1,128]{1,0:T(1,128)} %bitcast.71, s32[1,128]{1,0:T(1,128)} %bitcast.72, bf16[1,1024,384]{2,1,0:T(8,128)(2,1)} %wg_ref.1, ...), custom_call_target="tpu_custom_call" | custom-call | tf_op jit(solution)/shard_map/expert_layer/pallas_call | solution.py:284
  93.0 0.0 copy-done
  93.0 0.0 copy-done.1
  93.0 0.0 copy-done.3
  93.0 0.0 copy-start.2
  93.0 0.0 copy-start.4
  93.0 0.0 copy-start.5
  93.0 0.0 copy-start.6
  93.0 6.9 %fusion.19 = (f32[1,1024,384]{2,1,0:T(8,128)}, bf16[1,1024,384]{2,1,0:T(8,128)(2,1)}, f32[1,1024,384]{2,1,0:T(8,128)}, f32[1,1024,384]{2,1,0:T(8,128)}, bf16[1,1...) fusion(f32[1024,384]{1,0:T(8,128)} %get-tuple-element.16, f32[1,1024,384]{2,1,0:T(8,128)S(1)} %copy-done.3, ...), kind=kLoop, calls=%fused_computation.31 | loop fusion | flops 13369344 | bytes 18874368 | tf_op jit(solution)/shard_map/broadcast_in_dim | solution.py:348
  100.0 0.0 copy-done.2
  100.0 0.0 copy-done.4
  100.0 0.0 copy-done.5
  100.0 0.0 copy-done.6
  100.0 0.0 copy-start.7
  100.0 3.2 %fusion.18 = (f32[1,384,1024]{2,1,0:T(8,128)}, bf16[1,384,1024]{2,1,0:T(8,128)(2,1)}, f32[1,384,1024]{2,1,0:T(8,128)}) fusion(f32[384,1024]{1,0:T(8,128)S(1)} %copy-done.6, f32[1,384,1024]{2,1,0:T(8,128)S(1)} %copy-done.4, f32[1,384,1024]{2,1,0:T(8,128)S(1)} %copy-done.5, bf16[1,384,1024]{2,1,0:T(8,128)(2,1)S(1)} %copy-done.2), kind=kLoop, calls=%fused_computation.30 | loop fusion | flops 6684672 | bytes 9437184 | tf_op jit(solution)/shard_map/broadcast_in_dim | solution.py:349
  103.2 0.0 copy-done.7
  103.2 0.8 copy.24
Async XLA Ops:
  0.6 92.3 %copy-start = (bf16[1,1024,384]{2,1,0:T(8,128)(2,1)S(1)}, bf16[1,1024,384]{2,1,0:T(8,128)(2,1)}, u32[]{:S(2)}) copy-start(bf16[1,1024,384]{2,1,0:T(8,128)(2,1)} %wg_ref.1) | copy-start | bytes 2359300
  0.7 92.3 %copy-start.1 = (bf16[1,1024,384]{2,1,0:T(8,128)(2,1)S(1)}, bf16[1,1024,384]{2,1,0:T(8,128)(2,1)}, u32[]{:S(2)}) copy-start(bf16[1,1024,384]{2,1,0:T(8,128)(2,1)} %wu_ref.1) | copy-start | bytes 2359300
  0.7 92.3 %copy-start.3 = (f32[1,1024,384]{2,1,0:T(8,128)S(1)}, f32[1,1024,384]{2,1,0:T(8,128)}, u32[]{:S(2)}) copy-start(f32[1,1024,384]{2,1,0:T(8,128)} %param.24) | copy-start | bytes 4718596
  93.0 7.0 %copy-start.2 = (bf16[1,384,1024]{2,1,0:T(8,128)(2,1)S(1)}, bf16[1,384,1024]{2,1,0:T(8,128)(2,1)}, u32[]{:S(2)}) copy-start(bf16[1,384,1024]{2,1,0:T(8,128)(2,1)} %wd_ref.1) | copy-start | bytes 2359300
  93.0 7.0 %copy-start.4 = (f32[1,384,1024]{2,1,0:T(8,128)S(1)}, f32[1,384,1024]{2,1,0:T(8,128)}, u32[]{:S(2)}) copy-start(f32[1,384,1024]{2,1,0:T(8,128)} %param.25) | copy-start | bytes 4718596
  93.0 7.0 %copy-start.5 = (f32[1,384,1024]{2,1,0:T(8,128)S(1)}, f32[1,384,1024]{2,1,0:T(8,128)}, u32[]{:S(2)}) copy-start(f32[1,384,1024]{2,1,0:T(8,128)} %param.22) | copy-start | bytes 4718596
  93.0 7.0 %copy-start.6 = (f32[384,1024]{1,0:T(8,128)S(1)}, f32[384,1024]{1,0:T(8,128)}, u32[]{:S(2)}) copy-start(f32[384,1024]{1,0:T(8,128)} %get-tuple-element.17) | copy-start | bytes 4718596
  100.0 3.2 %copy-start.7 = (bf16[128,2048]{1,0:T(8,128)(2,1)S(1)}, bf16[128,2048]{1,0:T(8,128)(2,1)}, u32[]{:S(2)}) copy-start(bf16[128,2048]{1,0:T(8,128)(2,1)} %get-tuple-element.40) | copy-start | bytes 1572868

commit v4 on v3

--- a/solution.py
+++ b/solution.py
@@ -72,7 +72,7 @@
     near, far = list(range(half)), list(range(half, experts))
     order = near[:quarter] + far[:quarter] + near[quarter:] + far[quarter:]
     place = {k: pos for pos, k in enumerate(order)}
-    arrivals = near[1:3] + far[:2] + near[3:] + far[2:]
+    arrivals = near[1:quarter + 1] + far[:quarter] + near[quarter + 1:] + far[quarter:]
     window = 3
 
     def peer(k):
@@ -144,23 +144,13 @@
         for i in range(3):
             go(remote(weights[i], places(d)[i], ws.at[k - 1, i], wr.at[k - 1, i], {"dp": dp_at(k)}))
 
-    started = window
-    for k in arrivals:
-        pos = place[k]
-        for a in range(2):
-            remote(rows.at[a, 0, pos], rows.at[a, 0, pos], d_send.at[a, pos], d_recv.at[a, pos],
-                   peer(k)).wait_recv()
-            if k >= half and started < len(waiting):
-                direct(*waiting[started])
-                started += 1
-            forward(a, pos)
-
-    for copy in local:
-        copy.wait()
-    for k in range(1, n):
-        arriving = places(lax.rem(d + n - k, n))
-        for i in range(3):
-            remote(arriving[i], arriving[i], ws.at[k - 1, i], wr.at[k - 1, i], {"dp": dp_at(k)}).wait_recv()
+    def weights_here():
+        for copy in local:
+            copy.wait()
+        for k in range(1, n):
+            arriving = places(lax.rem(d + n - k, n))
+            for i in range(3):
+                remote(arriving[i], arriving[i], ws.at[k - 1, i], wr.at[k - 1, i], {"dp": dp_at(k)}).wait_recv()
 
     def through(b, lo, many):
         here = pl.ds(lo, many)
@@ -183,8 +173,26 @@
                 remote(rows.at[a, 1, pos], rows.at[a, 1, pos], f_send.at[a, pos], f_recv.at[a, pos],
                        {"expert": partner}).wait_recv()
         psend[pl.ds(lo, half)] = through(1, lo, half).astype(bf16)
+
+    def share(lo):
         for pos in list(range(lo + quarter, lo + half)) + list(range(lo, lo + quarter)):
             go(remote(psend.at[pos], precv.at[pos], p_send.at[pos], p_recv.at[pos], {"expert": partner}))
+
+    started = window
+    for k in arrivals:
+        pos = place[k]
+        for a in range(2):
+            remote(rows.at[a, 0, pos], rows.at[a, 0, pos], d_send.at[a, pos], d_recv.at[a, pos],
+                   peer(k)).wait_recv()
+            if k >= half and started < len(waiting):
+                direct(*waiting[started])
+                started += 1
+            forward(a, pos)
+        if k == half - 1:
+            weights_here()
+            part[pl.ds(0, half)] = through(0, 0, half)
+        if k == experts - 2:
+            forwarded(0)
 
     def weight_block(i):
         block = lax.rem((d + 1) * nb + i, n * nb)
@@ -212,11 +220,12 @@
             go(remote(rsend.at[pos], ret.at[e], r_send.at[pos], r_recv.at[pos], peer(k)))
 
     blocks = list(range(n * nb))
-    forwarded(0)
-    part[...] = through(0, 0, experts)
+    share(0)
+    part[pl.ds(half, half)] = through(0, half, half)
     for k in far[:quarter]:
         give_back(place[k])
     forwarded(half)
+    share(half)
     for k in near[1:quarter] + near[:1] + far[quarter:] + near[quarter:]:
         give_back(place[k])
         if blocks and k:

time: 104 us -> 105 us (level)
  no operation moved by 1% of the time
where the time goes in v4:
time: 105 us; the launch traced here: 104 us
  Pallas kernels  92.6 us (88%)
  other arithmetic  10.2 us (10%)
    pallas_call x1, Pallas kernels, expert_layer(): pl.pallas_call(functools.partial(kernel, n, experts, hot, bs), out_shape=...  92.6 us
    broadcast_in_dim x1, other arithmetic, per_device(): up_second[None]  6.93 us
    broadcast_in_dim x1, other arithmetic, per_device(): down_second[None]  3.23 us

profile of v4, /device:TPU:0, one launch (start us, length us, event | category | flops | bytes accessed | tf_op | source)
XLA Modules:
  0.0 104.4 jit_solution(9530191296948676748)
XLA Ops:
  0.6 0.0 copy-start
  0.7 0.0 copy-start.1
  0.7 0.0 copy-start.3
  0.7 92.6 %expert_layer.1 = (bf16[128,2048]{1,0:T(8,128)(2,1)}, f32[1024,384]{1,0:T(8,128)}, f32[1024,384]{1,0:T(8,128)}, f32[384,1024]{1,0:T(8,128)}) custom-call(bf16[128,2048]{1,0:T(8,128)(2,1)} %tok_ref.1, bf16[128,2048]{1,0:T(8,128)(2,1)} %og_ref.1, s32[1,128]{1,0:T(1,128)} %bitcast.71, s32[1,128]{1,0:T(1,128)} %bitcast.72, bf16[1,1024,384]{2,1,0:T(8,128)(2,1)} %wg_ref.1, ...), custom_call_target="tpu_custom_call" | custom-call | tf_op jit(solution)/shard_map/expert_layer/pallas_call | solution.py:293
  93.3 0.0 copy-done
  93.3 0.0 copy-done.1
  93.3 0.0 copy-done.3
  93.3 0.0 copy-start.2
  93.4 0.0 copy-start.4
  93.4 0.0 copy-start.5
  93.4 0.0 copy-start.6
  93.4 6.9 %fusion.19 = (f32[1,1024,384]{2,1,0:T(8,128)}, bf16[1,1024,384]{2,1,0:T(8,128)(2,1)}, f32[1,1024,384]{2,1,0:T(8,128)}, f32[1,1024,384]{2,1,0:T(8,128)}, bf16[1,1...) fusion(f32[1024,384]{1,0:T(8,128)} %get-tuple-element.16, f32[1,1024,384]{2,1,0:T(8,128)S(1)} %copy-done.3, ...), kind=kLoop, calls=%fused_computation.31 | loop fusion | flops 13369344 | bytes 18874368 | tf_op jit(solution)/shard_map/broadcast_in_dim | solution.py:357
  100.3 0.0 copy-done.2
  100.3 0.0 copy-done.4
  100.3 0.0 copy-done.5
  100.4 0.0 copy-done.6
  100.4 0.0 copy-start.7
  100.4 3.2 %fusion.18 = (f32[1,384,1024]{2,1,0:T(8,128)}, bf16[1,384,1024]{2,1,0:T(8,128)(2,1)}, f32[1,384,1024]{2,1,0:T(8,128)}) fusion(f32[384,1024]{1,0:T(8,128)S(1)} %copy-done.6, f32[1,384,1024]{2,1,0:T(8,128)S(1)} %copy-done.4, f32[1,384,1024]{2,1,0:T(8,128)S(1)} %copy-done.5, bf16[1,384,1024]{2,1,0:T(8,128)(2,1)S(1)} %copy-done.2), kind=kLoop, calls=%fused_computation.30 | loop fusion | flops 6684672 | bytes 9437184 | tf_op jit(solution)/shard_map/broadcast_in_dim | solution.py:358
  103.6 0.0 copy-done.7
  103.6 0.8 copy.24
Async XLA Ops:
  0.6 92.7 %copy-start = (bf16[1,1024,384]{2,1,0:T(8,128)(2,1)S(1)}, bf16[1,1024,384]{2,1,0:T(8,128)(2,1)}, u32[]{:S(2)}) copy-start(bf16[1,1024,384]{2,1,0:T(8,128)(2,1)} %wg_ref.1) | copy-start | bytes 2359300
  0.7 92.7 %copy-start.1 = (bf16[1,1024,384]{2,1,0:T(8,128)(2,1)S(1)}, bf16[1,1024,384]{2,1,0:T(8,128)(2,1)}, u32[]{:S(2)}) copy-start(bf16[1,1024,384]{2,1,0:T(8,128)(2,1)} %wu_ref.1) | copy-start | bytes 2359300
  0.7 92.7 %copy-start.3 = (f32[1,1024,384]{2,1,0:T(8,128)S(1)}, f32[1,1024,384]{2,1,0:T(8,128)}, u32[]{:S(2)}) copy-start(f32[1,1024,384]{2,1,0:T(8,128)} %param.24) | copy-start | bytes 4718596
  93.3 7.0 %copy-start.2 = (bf16[1,384,1024]{2,1,0:T(8,128)(2,1)S(1)}, bf16[1,384,1024]{2,1,0:T(8,128)(2,1)}, u32[]{:S(2)}) copy-start(bf16[1,384,1024]{2,1,0:T(8,128)(2,1)} %wd_ref.1) | copy-start | bytes 2359300
  93.4 7.0 %copy-start.4 = (f32[1,384,1024]{2,1,0:T(8,128)S(1)}, f32[1,384,1024]{2,1,0:T(8,128)}, u32[]{:S(2)}) copy-start(f32[1,384,1024]{2,1,0:T(8,128)} %param.25) | copy-start | bytes 4718596
  93.4 7.0 %copy-start.5 = (f32[1,384,1024]{2,1,0:T(8,128)S(1)}, f32[1,384,1024]{2,1,0:T(8,128)}, u32[]{:S(2)}) copy-start(f32[1,384,1024]{2,1,0:T(8,128)} %param.22) | copy-start | bytes 4718596
  93.4 7.0 %copy-start.6 = (f32[384,1024]{1,0:T(8,128)S(1)}, f32[384,1024]{1,0:T(8,128)}, u32[]{:S(2)}) copy-start(f32[384,1024]{1,0:T(8,128)} %get-tuple-element.17) | copy-start | bytes 4718596
  100.4 3.2 %copy-start.7 = (bf16[128,2048]{1,0:T(8,128)(2,1)S(1)}, bf16[128,2048]{1,0:T(8,128)(2,1)}, u32[]{:S(2)}) copy-start(bf16[128,2048]{1,0:T(8,128)(2,1)} %get-tuple-element.40) | copy-start | bytes 1572868
